TPU v7x, 32 devices: a whole 2x2x4 slice. The times are simulated.
32 devices in a mesh: groups: 2 (over x), mp: 8 (over z, y), dp: 2 (over core).
Axes of the slice: x: 2, y: 2, z: 4, core: 2. Of those that a mesh axis runs over, the one named last changes fastest.
Arguments:
- latents: bfloat16 [12, 128, 128, 320], P(('groups', 'dp'), 'mp'), parts along dimension 0, may hold values from -6 to 6
- room_labels: int32 [12, 128, 128], P(('groups', 'dp'), 'mp'), parts along dimension 0, may hold values from 0 to 15
- timesteps: int32 [12], P(('groups', 'dp')), parts along dimension 0, may hold values from 0 to 999
- label_table: bfloat16 [16, 320], replicated, may hold values from -6 to 6
- time_weight: bfloat16 [1280, 320], replicated, may hold values from -0.15625 to 0.15625
- trunk_weight: bfloat16 [320, 3, 3, 320], P('mp'), may hold values from -0.109375 to 0.109375
- control_weight: bfloat16 [320, 3, 3, 320], P('mp'), may hold values from -0.109375 to 0.109375
- mix_weight: bfloat16 [320, 320], P('mp'), may hold values from -0.3125 to 0.3125
- cotangent: bfloat16 [12, 128, 128, 320], P(('groups', 'dp'), 'mp'), parts along dimension 0, may hold values from -0.08984375 to 0.08984375
Outputs:
- output: bfloat16 [12, 128, 128, 320], P(('groups', 'dp'), 'mp'), parts along dimension 0
- grad_control: float32 [640, 3, 3, 320], P(('groups', 'mp')), parts along dimension 0
- grad_mix: float32 [640, 320], P(('groups', 'mp')), parts along dimension 0
- grad_table: float32 [32, 320], P('groups'), parts along dimension 0
There are 2 independent parts, one for each index of `groups`. A program takes and returns all parts, laid end to end along the dimension named above; an argument that names none is the same for every part. Nothing has to cross between parts.
All inputs are finite; a program needn't handle non-finite values.
Results may differ from a plain program's by a relative error of at most 0.0057.
Values may be sent and summed in bfloat16 or wider, within the bound.
A program may use at most 256 MiB of HBM per device.

v0:
```python
import math
import jax
import jax.numpy as jnp
from jax import lax
from jax.sharding import PartitionSpec as P


def with_halo(cells, sides, width):
    for axis, dim in sides:
        count = lax.axis_size(axis)
        ends = count - 1
        head = lax.slice_in_dim(cells, 0, width, axis=dim)
        tail = lax.slice_in_dim(cells, cells.shape[dim] - width, cells.shape[dim], axis=dim)
        cells = jnp.concatenate(
            [
                lax.ppermute(tail, axis, [(i, (i + 1) % count) for i in range(ends)]),
                cells,
                lax.ppermute(head, axis, [((i + 1) % count, i) for i in range(ends)]),
            ],
            axis=dim,
        )
    return cells


def sinusoid(timesteps, embed_width):
    half_width = embed_width // 2
    indices = jnp.arange(half_width, dtype=jnp.float32)
    frequency = jnp.exp(-math.log(10000.0) * indices / half_width)
    angles = timesteps.astype(jnp.float32)[:, None] * frequency[None, :]
    return jnp.concatenate([jnp.cos(angles), jnp.sin(angles)], axis=1)


def forward_taps(frame, kernel):
    row_count = frame.shape[1] - 2
    span_cols = frame.shape[2] - 2
    running = jnp.zeros(frame.shape[:1] + (row_count, span_cols, kernel.shape[3]), jnp.float32)
    for tap_row in range(3):
        for tap_col in range(3):
            running = running + jnp.einsum(
                "bhwc,cd->bhwd",
                frame[:, tap_row : tap_row + row_count, tap_col : tap_col + span_cols],
                kernel[:, tap_row, tap_col],
                preferred_element_type=jnp.float32,
            )
    return running


def backward_taps(frame, kernel):
    row_count = frame.shape[1] - 2
    span_cols = frame.shape[2] - 2
    running = jnp.zeros(frame.shape[:1] + (row_count, span_cols, kernel.shape[0]), jnp.float32)
    for tap_row in range(3):
        for tap_col in range(3):
            running = running + jnp.einsum(
                "bhwd,cd->bhwc",
                frame[
                    :, 2 - tap_row : 2 - tap_row + row_count, 2 - tap_col : 2 - tap_col + span_cols
                ],
                kernel[:, tap_row, tap_col],
                preferred_element_type=jnp.float32,
            )
    return running


def per_device(
    latents,
    room_labels,
    timesteps,
    label_table,
    time_weight,
    trunk_weight,
    control_weight,
    mix_weight,
    cotangent,
):
    images, row_count, span_cols, channels = latents.shape
    rooms = label_table.shape[0]
    onehot = (room_labels[..., None] == jnp.arange(rooms, dtype=jnp.int32)).astype(jnp.bfloat16)
    embedded = jnp.einsum("bhwr,rc->bhwc", onehot, label_table, preferred_element_type=jnp.float32)
    control_in = (latents.astype(jnp.float32) + embedded).astype(jnp.bfloat16)
    stacked = jnp.stack([latents, control_in])
    framed = with_halo(stacked, (("mp", 2),), 1)
    framed = jnp.pad(framed, ((0, 0), (0, 0), (0, 0), (1, 1), (0, 0)))
    trunk_frame = framed[0]
    control_frame = framed[1]
    time_features = jax.nn.silu(sinusoid(timesteps, time_weight.shape[0])).astype(jnp.bfloat16)
    time_shift = jnp.dot(time_features, time_weight, preferred_element_type=jnp.float32)[
        :, None, None, :
    ]
    trunk_full = lax.all_gather(trunk_weight, "mp", axis=0, tiled=True)
    trunk_pre = forward_taps(trunk_frame, trunk_full) + time_shift
    control_full, mix_full = (
        lax.all_gather(control_weight, "mp", axis=0, tiled=True),
        lax.all_gather(mix_weight, "mp", axis=0, tiled=True),
    )
    control_pre = forward_taps(control_frame, control_full) + time_shift
    gated_act = jax.nn.silu(control_pre).astype(jnp.bfloat16)
    mixed_out = jnp.einsum("bhwc,cd->bhwd", gated_act, mix_full, preferred_element_type=jnp.float32)
    output = (jax.nn.silu(trunk_pre) + mixed_out).astype(jnp.bfloat16)
    back_gate = jnp.einsum("bhwd,cd->bhwc", cotangent, mix_full, preferred_element_type=jnp.float32)
    sigmoid_val = jax.nn.sigmoid(control_pre)
    back_pre = (back_gate * sigmoid_val * (1.0 + control_pre * (1.0 - sigmoid_val))).astype(
        jnp.bfloat16
    )
    back_frame = with_halo(back_pre, (("mp", 1),), 1)
    back_frame = jnp.pad(back_frame, ((0, 0), (0, 0), (1, 1), (0, 0)))
    back_kernel = lax.all_gather(control_weight, "mp", axis=0, tiled=True)
    back_in = backward_taps(back_frame, back_kernel)
    table_local = jnp.einsum(
        "bhwr,bhwc->rc", onehot.astype(jnp.float32), back_in, precision=lax.Precision.HIGHEST
    )
    grad_table = lax.psum(table_local, ("mp", "dp"))
    pieces = []
    for tap_row in range(3):
        for tap_col in range(3):
            pieces.append(
                jnp.einsum(
                    "bhwc,bhwd->cd",
                    control_frame[:, tap_row : tap_row + row_count, tap_col : tap_col + span_cols],
                    back_pre,
                    preferred_element_type=jnp.float32,
                )
            )
    kernel_rows = jnp.stack(pieces, axis=1).reshape(channels, 9 * channels)
    mix_rows = jnp.einsum("bhwc,bhwd->cd", gated_act, cotangent, preferred_element_type=jnp.float32)
    grad_term = jnp.concatenate([kernel_rows, mix_rows], axis=1)
    grad_rows = lax.psum_scatter(grad_term, "mp", scatter_dimension=0, tiled=True)
    grad_rows = lax.psum(grad_rows, "dp")
    grad_control = grad_rows[:, : 9 * channels].reshape(grad_rows.shape[0], 3, 3, channels)
    grad_mix = grad_rows[:, 9 * channels :]
    return (output, grad_control, grad_mix, grad_table)


def solution(mesh):
    in_specs = (
        P(("groups", "dp"), "mp", None, None),
        P(("groups", "dp"), "mp", None),
        P(("groups", "dp")),
        P(),
        P(),
        P("mp", None, None, None),
        P("mp", None, None, None),
        P("mp", None),
        P(("groups", "dp"), "mp", None, None),
    )
    out_specs = (
        P(("groups", "dp"), "mp", None, None),
        P(("groups", "mp"), None, None, None),
        P(("groups", "mp"), None),
        P("groups", None),
    )
    return jax.shard_map(
        per_device, mesh=mesh, in_specs=in_specs, out_specs=out_specs, check_vma=False
    )
```

profile of v0, /device:TPU:0, one launch (start us, length us, event | category | flops | bytes accessed | tf_op | source)
XLA Modules:
  0.0 456.9 jit_solution(16254729280796380880)
XLA Ops:
  8.0 3.5 fusion.27
  13.5 4.9 %collective-permute-start = (bf16[2,3,1,128,320]{3,4,2,1,0:T(8,128)(2,1)S(1)}, bf16[2,3,1,128,320]{3,4,2,1,0:T(8,128)(2,1)S(1)}, u32[]{:S(2)}, u32[]{:S(2)}) collective-permute-start(bf16[2,3,1,128,320]{3,4,2,1,0:T(8,128)(2,1)S(1)} %get-tuple-element.14), channel_id=1, source_target_pairs={{0,2},{2,4},{4,6},{6,8},{8,10},{10,12},{12,14},{1,3},{3,5},{5,7},{... | collective-permute-start | bytes 1474568 | tf_op jit(solution)/shard_map/ppermute | solution.py:16
  19.7 49.6 %all_gather.12 = bf16[320,320]{1,0:T(8,128)(2,1)S(1)} all-gather(bf16[40,320]{1,0:T(8,128)(2,1)S(1)} %copy-done.13), channel_id=1, replica_groups=mesh['groups'=2,'mp'=8,'dp'=2] {'mp'}, dimensions={0}, use_global_device_ids=true | all-gather | bytes 230400 | tf_op jit(solution)/shard_map/all_gather | solution.py:94
  69.9 18.2 %select_maximum_fusion = bf16[2,3,18,130,320]{3,4,2,1,0:T(8,128)(2,1)S(1)} fusion(bf16[2,3,1,128,320]{3,4,2,1,0:T(8,128)(2,1)S(1)} %collective-permute-done.1, bf16[2,3,1,128,320]{3,4,2,1,0:T(8,128)(2,1)S(1)} %collective-permute-done, bf16[1,3,16,128,320]{3,4,2,1,0:T(8,128)(2,1)} %copy-done.6, bf16[1,3,16,128,320]{3,4,2,1,0:T(8,128)(2,1)} %bitcast.302), kind=kLoop, calls=%fused_computation.5 | loop fusion | flops 67392000 | bytes 17832960 | tf_op jit(solution)/shard_map/concatenate | solution.py:14
  88.1 6.6 %slice_bitcast_fusion.1 = (bf16[3,18,130,320]{2,3,1,0:T(8,128)(2,1)}, bf16[3,18,130,320]{2,3,1,0:T(8,128)(2,1)}) fusion(bf16[2,3,18,130,320]{3,4,2,1,0:T(8,128)(2,1)S(1)} %select_maximum_fusion), kind=kLoop, calls=%fused_computation.17 | loop fusion | bytes 17971200 | tf_op jit(solution)/shard_map/squeeze | solution.py:84
  94.7 9.1 %fusion.64 = f32[3,16,128,320]{2,3,1,0:T(8,128)} fusion(bf16[3,18,130,320]{2,3,1,0:T(8,128)(2,1)} %get-tuple-element.13, bf16[320,3,3,320]{3,0,2,1:T(8,128)(2,1)} %all-gather.5.cloned.1.call-done), kind=kOutput, calls=%fused_computation.79 | convolution fusion | flops 1258291200 | bytes 12042240 | tf_op jit(solution)/shard_map/bhwc,cd->bhwd/dot_general | solution.py:39
  103.8 5.3 %fusion.68 = f32[3,16,128,320]{2,3,1,0:T(8,128)} fusion(bf16[3,18,130,320]{2,3,1,0:T(8,128)(2,1)S(1)} %copy-done.2, bf16[320,3,3,320]{3,0,2,1:T(8,128)(2,1)S(1)} %copy-done.9), kind=kOutput, calls=%fused_computation.83 | convolution fusion | flops 1258291200 | bytes 12042240 | tf_op jit(solution)/shard_map/bhwc,cd->bhwd/dot_general | solution.py:39
  109.1 5.5 %fusion.72 = f32[3,16,128,320]{2,3,1,0:T(8,128)} fusion(bf16[3,18,130,320]{2,3,1,0:T(8,128)(2,1)S(1)} %copy-done.2, bf16[320,3,3,320]{3,0,2,1:T(8,128)(2,1)S(1)} %copy-done.9), kind=kOutput, calls=%fused_computation.87 | convolution fusion | flops 1258291200 | bytes 12042240 | tf_op jit(solution)/shard_map/bhwc,cd->bhwd/dot_general | solution.py:39
  114.6 5.5 %fusion.76 = f32[3,16,128,320]{2,3,1,0:T(8,128)} fusion(bf16[3,18,130,320]{2,3,1,0:T(8,128)(2,1)S(1)} %copy-done.2, bf16[320,3,3,320]{3,0,2,1:T(8,128)(2,1)S(1)} %copy-done.9), kind=kOutput, calls=%fused_computation.91 | convolution fusion | flops 1258291200 | bytes 12042240 | tf_op jit(solution)/shard_map/bhwc,cd->bhwd/dot_general | solution.py:39
  120.2 5.3 %fusion.80 = f32[3,16,128,320]{2,3,1,0:T(8,128)} fusion(bf16[3,18,130,320]{2,3,1,0:T(8,128)(2,1)S(1)} %copy-done.2, bf16[320,3,3,320]{3,0,2,1:T(8,128)(2,1)S(1)} %copy-done.9), kind=kOutput, calls=%fused_computation.95 | convolution fusion | flops 1258291200 | bytes 12042240 | tf_op jit(solution)/shard_map/bhwc,cd->bhwd/dot_general | solution.py:39
  125.5 5.8 %fusion.84 = f32[3,16,128,320]{2,3,1,0:T(8,128)} fusion(bf16[3,18,130,320]{2,3,1,0:T(8,128)(2,1)S(1)} %copy-done.2, bf16[320,3,3,320]{3,0,2,1:T(8,128)(2,1)S(1)} %copy-done.9), kind=kOutput, calls=%fused_computation.99 | convolution fusion | flops 1258291200 | bytes 12042240 | tf_op jit(solution)/shard_map/bhwc,cd->bhwd/dot_general | solution.py:39
  131.3 5.7 %fusion.88 = f32[3,16,128,320]{2,3,1,0:T(8,128)} fusion(bf16[3,18,130,320]{2,3,1,0:T(8,128)(2,1)S(1)} %copy-done.2, bf16[320,3,3,320]{3,0,2,1:T(8,128)(2,1)S(1)} %copy-done.9), kind=kOutput, calls=%fused_computation.103 | convolution fusion | flops 1258291200 | bytes 12042240 | tf_op jit(solution)/shard_map/bhwc,cd->bhwd/dot_general | solution.py:39
  137.0 5.4 %fusion.92 = f32[3,16,128,320]{2,3,1,0:T(8,128)} fusion(bf16[3,18,130,320]{2,3,1,0:T(8,128)(2,1)S(1)} %copy-done.2, bf16[320,3,3,320]{3,0,2,1:T(8,128)(2,1)S(1)} %copy-done.9), kind=kOutput, calls=%fused_computation.107 | convolution fusion | flops 1258291200 | bytes 12042240 | tf_op jit(solution)/shard_map/bhwc,cd->bhwd/dot_general | solution.py:39
  142.4 28.2 %multiply_convert_fusion.1 = (bf16[3,16,128,320]{2,3,1,0:T(8,128)(2,1)}, f32[3,16,128,320]{2,3,1,0:T(8,128)}) fusion(f32[3,320]{1,0:T(4,128)S(1)} %fusion.163, bf16[3,18,130,320]{2,3,1,0:T(8,128)(2,1)} %get-tuple-element.13, bf16[320,3,3,320]{3,0,2,1:T(8,128)(2,1)S(1)} %copy-done.9, f32[3,16,128,320]{2,3,1,0:T(8,128)} %fusion.64, ...), kind=kOutput, calls=%fused_computation.29 | convolution fusion | flops 1285816320 | bytes 78895104 | tf_op jit(solution)/shard_map/bhwc,cd->bhwd/dot_general | solution.py:39
  170.6 7.3 %multiply_convert_fusion = bf16[3,16,128,320]{2,3,1,0:T(8,128)(2,1)S(1)} fusion(f32[3,16,128,320]{2,3,1,0:T(8,128)} %get-tuple-element.21, bf16[3,16,128,320]{2,3,1,0:T(8,128)(2,1)} %param.17, bf16[320,320]{1,0:T(8,128)(2,1)S(1)} %all_gather.12), kind=kOutput, calls=%fused_computation.27 | convolution fusion | flops 1275985920 | bytes 15933440 | tf_op jit(solution)/shard_map/bhwd,cd->bhwc/dot_general | solution.py:100
  178.0 5.7 %fusion.101 = f32[320,9,320]{0,2,1:T(8,128)S(1)} fusion(bf16[3,16,128,320]{2,3,1,0:T(8,128)(2,1)S(1)} %multiply_convert_fusion, bf16[3,18,130,320]{2,3,1,0:T(8,128)(2,1)} %get-tuple-element.13), kind=kOutput, calls=%fused_computation.110 | convolution fusion | flops 1258291200 | bytes 8355840 | tf_op jit(solution)/shard_map/bhwc,bhwd->cd/dot_general | solution.py:117
  187.0 5.5 %fusion.107 = f32[320,9,320]{0,2,1:T(8,128)S(1)} fusion(f32[320,9,320]{0,2,1:T(8,128)S(1)} %fusion.101, bf16[3,16,128,320]{2,3,1,0:T(8,128)(2,1)S(1)} %multiply_convert_fusion, bf16[3,18,130,320]{2,3,1,0:T(8,128)(2,1)} %get-tuple-element.13), kind=kOutput, calls=%fused_computation.112 | convolution fusion | flops 1258291200 | bytes 8355840 | tf_op jit(solution)/shard_map/bhwc,bhwd->cd/dot_general | solution.py:117
  192.5 2.3 fusion.113
  194.8 2.2 fusion.119
  197.0 2.3 fusion.125
  199.3 2.3 fusion.131
  201.6 2.2 fusion.137
  203.8 2.5 fusion.143
  206.3 2.3 fusion.149
  210.8 5.6 %copy.38 = f32[320,2880]{1,0:T(8,128)} copy(f32[320,2880]{0,1:T(8,128)} %bitcast.304) | data formatting | bytes 7372800 | tf_op jit(solution)/shard_map/reshape | solution.py:124
  216.4 7.6 %fusion.156 = f32[3,16,128,320]{2,3,1,0:T(8,128)} fusion(bf16[3,16,128,320]{2,3,1,0:T(8,128)(2,1)} %get-tuple-element.20, bf16[320,320]{1,0:T(8,128)(2,1)S(1)} %all_gather.12), kind=kOutput, calls=%fused_computation.151 | convolution fusion | flops 1258291200 | bytes 12001280 | tf_op jit(solution)/shard_map/bhwc,cd->bhwd/dot_general | solution.py:98
  226.2 2.3 pad_maximum_fusion
  228.7 9.0 %fusion.42 = f32[3,16,128,320]{2,3,1,0:T(8,128)} fusion(bf16[3,18,130,320]{2,3,1,0:T(8,128)(2,1)} %get-tuple-element.12, bf16[320,3,3,320]{3,0,2,1:T(8,128)(2,1)} %all-gather.3.cloned.1.call-done), kind=kOutput, calls=%fused_computation.57 | convolution fusion | flops 1258291200 | bytes 12042240 | tf_op jit(solution)/shard_map/bhwc,cd->bhwd/dot_general | solution.py:39
  237.7 7.5 %fusion.44 = f32[3,16,128,320]{2,3,1,0:T(8,128)} fusion(bf16[3,18,130,320]{2,3,1,0:T(8,128)(2,1)} %get-tuple-element.12, bf16[320,3,3,320]{3,0,2,1:T(8,128)(2,1)S(1)} %copy-done.11), kind=kOutput, calls=%fused_computation.59 | convolution fusion | flops 1258291200 | bytes 12042240 | tf_op jit(solution)/shard_map/bhwc,cd->bhwd/dot_general | solution.py:39
  245.2 5.5 %fusion.46 = f32[3,16,128,320]{2,3,1,0:T(8,128)} fusion(bf16[3,18,130,320]{2,3,1,0:T(8,128)(2,1)S(1)} %bitcast.299, bf16[320,3,3,320]{3,0,2,1:T(8,128)(2,1)S(1)} %copy-done.11), kind=kOutput, calls=%fused_computation.61 | convolution fusion | flops 1258291200 | bytes 12042240 | tf_op jit(solution)/shard_map/bhwc,cd->bhwd/dot_general | solution.py:39
  250.7 5.6 %fusion.48 = f32[3,16,128,320]{2,3,1,0:T(8,128)} fusion(bf16[3,18,130,320]{2,3,1,0:T(8,128)(2,1)S(1)} %bitcast.299, bf16[320,3,3,320]{3,0,2,1:T(8,128)(2,1)S(1)} %copy-done.11), kind=kOutput, calls=%fused_computation.63 | convolution fusion | flops 1258291200 | bytes 12042240 | tf_op jit(solution)/shard_map/bhwc,cd->bhwd/dot_general | solution.py:39
  256.3 5.3 %fusion.50 = f32[3,16,128,320]{2,3,1,0:T(8,128)} fusion(bf16[3,18,130,320]{2,3,1,0:T(8,128)(2,1)S(1)} %bitcast.299, bf16[320,3,3,320]{3,0,2,1:T(8,128)(2,1)S(1)} %copy-done.11), kind=kOutput, calls=%fused_computation.65 | convolution fusion | flops 1258291200 | bytes 12042240 | tf_op jit(solution)/shard_map/bhwc,cd->bhwd/dot_general | solution.py:39
  261.6 6.0 %fusion.52 = f32[3,16,128,320]{2,3,1,0:T(8,128)} fusion(bf16[3,18,130,320]{2,3,1,0:T(8,128)(2,1)S(1)} %bitcast.299, bf16[320,3,3,320]{3,0,2,1:T(8,128)(2,1)S(1)} %copy-done.11), kind=kOutput, calls=%fused_computation.67 | convolution fusion | flops 1258291200 | bytes 12042240 | tf_op jit(solution)/shard_map/bhwc,cd->bhwd/dot_general | solution.py:39
  267.6 5.6 %fusion.54 = f32[3,16,128,320]{2,3,1,0:T(8,128)} fusion(bf16[3,18,130,320]{2,3,1,0:T(8,128)(2,1)S(1)} %bitcast.299, bf16[320,3,3,320]{3,0,2,1:T(8,128)(2,1)S(1)} %copy-done.11), kind=kOutput, calls=%fused_computation.69 | convolution fusion | flops 1258291200 | bytes 12042240 | tf_op jit(solution)/shard_map/bhwc,cd->bhwd/dot_general | solution.py:39
  273.2 5.3 %fusion.56 = f32[3,16,128,320]{2,3,1,0:T(8,128)} fusion(bf16[3,18,130,320]{2,3,1,0:T(8,128)(2,1)S(1)} %bitcast.299, bf16[320,3,3,320]{3,0,2,1:T(8,128)(2,1)S(1)} %copy-done.11), kind=kOutput, calls=%fused_computation.71 | convolution fusion | flops 1258291200 | bytes 12042240 | tf_op jit(solution)/shard_map/bhwc,cd->bhwd/dot_general | solution.py:39
  278.5 28.6 %add_convert_fusion = bf16[3,16,128,320]{2,3,1,0:T(8,128)(2,1)} fusion(f32[3,16,128,320]{2,3,1,0:T(8,128)} %fusion.156, f32[3,16,128,320]{2,3,1,0:T(8,128)} %fusion.42, f32[3,16,128,320]{2,3,1,0:T(8,128)} %fusion.44, f32[3,16,128,320]{2,3,1,0:T(8,128)} %fusion.46, f32[3,16,128,320]{2,3,1,0:T(8,128)} %fusion.48, f32[3,16,128,320]{2,3,1,0:T(8,128)} %fusion.50, ...), kind=kOutput, calls=%fused_computation.28 | convolution fusion | flops 1287782400 | bytes 78892800 | tf_op jit(solution)/shard_map/bhwc,cd->bhwd/dot_general | solution.py:39
  307.2 7.6 %fusion.158 = f32[3,16,128,320]{2,3,1,0:T(8,128)} fusion(bf16[3,16,128,320]{2,3,1,0:T(8,128)(2,1)} %copy-done.3, bf16[320,3,3,320]{3,0,2,1:T(8,128)(2,1)S(1)} %copy-done.9), kind=kOutput, calls=%fused_computation.153 | convolution fusion | flops 1258291200 | bytes 12042240 | tf_op jit(solution)/shard_map/bhwd,cd->bhwc/dot_general | solution.py:54
  314.8 5.3 %fusion.19 = f32[3,16,128,320]{2,3,1,0:T(8,128)} fusion(bf16[3,1,128,320]{2,3,1,0:T(8,128)(2,1)S(1)} %collective-permute-done.3, bf16[3,16,128,320]{2,3,1,0:T(8,128)(2,1)S(1)} %copy-done.4, bf16[320,3,3,320]{3,0,2,1:T(8,128)(2,1)S(1)} %copy-done.9), kind=kOutput, calls=%fused_computation.33 | convolution fusion | flops 1266647040 | bytes 12288000 | tf_op jit(solution)/shard_map/bhwd,cd->bhwc/dot_general | solution.py:54
  320.1 5.3 %fusion.23 = f32[3,16,128,320]{2,3,1,0:T(8,128)} fusion(bf16[3,16,128,320]{2,3,1,0:T(8,128)(2,1)S(1)} %copy-done.4, bf16[3,1,128,320]{2,3,1,0:T(8,128)(2,1)S(1)} %collective-permute-done.2, bf16[320,3,3,320]{3,0,2,1:T(8,128)(2,1)S(1)} %copy-done.9), kind=kOutput, calls=%fused_computation.37 | convolution fusion | flops 1266647040 | bytes 12288000 | tf_op jit(solution)/shard_map/bhwd,cd->bhwc/dot_general | solution.py:54
  325.4 6.3 %fusion.9 = bf16[3,18,130,320]{2,3,1,0:T(8,128)(2,1)S(1)} fusion(bf16[3,1,128,320]{2,3,1,0:T(8,128)(2,1)S(1)} %collective-permute-done.3, bf16[3,16,128,320]{2,3,1,0:T(8,128)(2,1)S(1)} %copy-done.4, bf16[3,1,128,320]{2,3,1,0:T(8,128)(2,1)S(1)} %collective-permute-done.2), kind=kLoop, calls=%fused_computation.15 | loop fusion | flops 26956800 | bytes 8916480 | tf_op jit(solution)/shard_map/concatenate | solution.py:14
  331.8 5.5 %fusion.30 = f32[3,16,128,320]{2,3,1,0:T(8,128)} fusion(bf16[3,18,130,320]{2,3,1,0:T(8,128)(2,1)S(1)} %fusion.9, bf16[320,3,3,320]{3,0,2,1:T(8,128)(2,1)S(1)} %copy-done.9), kind=kOutput, calls=%fused_computation.45 | convolution fusion | flops 1258291200 | bytes 12042240 | tf_op jit(solution)/shard_map/bhwd,cd->bhwc/dot_general | solution.py:54
  337.3 5.3 %fusion.32 = f32[3,16,128,320]{2,3,1,0:T(8,128)} fusion(bf16[3,18,130,320]{2,3,1,0:T(8,128)(2,1)S(1)} %fusion.9, bf16[320,3,3,320]{3,0,2,1:T(8,128)(2,1)S(1)} %copy-done.9), kind=kOutput, calls=%fused_computation.47 | convolution fusion | flops 1258291200 | bytes 12042240 | tf_op jit(solution)/shard_map/bhwd,cd->bhwc/dot_general | solution.py:54
  342.7 5.5 %fusion.34 = f32[3,16,128,320]{2,3,1,0:T(8,128)} fusion(bf16[3,18,130,320]{2,3,1,0:T(8,128)(2,1)S(1)} %fusion.9, bf16[320,3,3,320]{3,0,2,1:T(8,128)(2,1)S(1)} %copy-done.9), kind=kOutput, calls=%fused_computation.49 | convolution fusion | flops 1258291200 | bytes 12042240 | tf_op jit(solution)/shard_map/bhwd,cd->bhwc/dot_general | solution.py:54
  348.2 5.4 %fusion.36 = f32[3,16,128,320]{2,3,1,0:T(8,128)} fusion(bf16[3,18,130,320]{2,3,1,0:T(8,128)(2,1)S(1)} %fusion.9, bf16[320,3,3,320]{3,0,2,1:T(8,128)(2,1)S(1)} %copy-done.9), kind=kOutput, calls=%fused_computation.51 | convolution fusion | flops 1258291200 | bytes 12042240 | tf_op jit(solution)/shard_map/bhwd,cd->bhwc/dot_general | solution.py:54
  353.6 5.5 %fusion.38 = f32[3,16,128,320]{2,3,1,0:T(8,128)} fusion(bf16[3,18,130,320]{2,3,1,0:T(8,128)(2,1)S(1)} %fusion.9, bf16[320,3,3,320]{3,0,2,1:T(8,128)(2,1)S(1)} %copy-done.9), kind=kOutput, calls=%fused_computation.53 | convolution fusion | flops 1258291200 | bytes 12042240 | tf_op jit(solution)/shard_map/bhwd,cd->bhwc/dot_general | solution.py:54
  359.0 5.3 %fusion.28 = f32[3,16,128,320]{2,3,1,0:T(8,128)} fusion(bf16[3,18,130,320]{2,3,1,0:T(8,128)(2,1)S(1)} %fusion.9, bf16[320,3,3,320]{3,0,2,1:T(8,128)(2,1)S(1)} %copy-done.9), kind=kOutput, calls=%fused_computation.43 | convolution fusion | flops 1258291200 | bytes 12042240 | tf_op jit(solution)/shard_map/bhwd,cd->bhwc/dot_general | solution.py:54
  364.4 24.3 %fusion.152 = f32[16,320]{1,0:T(8,128)S(1)} fusion(f32[3,16,128,320]{2,3,1,0:T(8,128)} %fusion.28, f32[3,16,128,320]{2,3,1,0:T(8,128)} %fusion.23, f32[3,16,128,320]{2,3,1,0:T(8,128)} %fusion.30, f32[3,16,128,320]{2,3,1,0:T(8,128)} %fusion.32, f32[3,16,128,320]{2,3,1,0:T(8,128)} %fusion.158, f32[3,16,128,320]{2,3,1,0:T(8,128)} %fusion.34, ...), kind=kOutput, calls=%fused_computation.128 | convolution fusion | flops 393314304 | bytes 70823936 | tf_op jit(solution)/shard_map/bhwr,bhwc->rc/dot_general | solution.py:109
  388.7 57.6 %psum.15 = f32[16,320]{1,0:T(8,128)} all-reduce(f32[16,320]{1,0:T(8,128)S(1)} %fusion.152), channel_id=1, replica_groups=mesh['groups'=2,'mp'=8,'dp'=2] {'mp','dp'}, use_global_device_ids=true, to_apply=%region_2.3 | all-reduce | flops 5120 | bytes 40960 | tf_op jit(solution)/shard_map/psum | solution.py:112
  (76 shorter events, 16.2 us)
Async XLA Ops:
  7.2 62.4 %copy-start = (bf16[1280,320]{0,1:T(8,128)(2,1)S(1)}, bf16[1280,320]{0,1:T(8,128)(2,1)}, u32[]{:S(2)}) copy-start(bf16[1280,320]{0,1:T(8,128)(2,1)} %param.13) | copy-start | bytes 2457604
  7.2 87.5 %all-gather.5.cloned.1.call-start = ((), (), s32[]{:S(2)}) async-start(), calls=%async_computation.2 | async-start | bytes 2488320 | tf_op jit(solution)/shard_map/all_gather | solution.py:93
  7.9 11.8 %copy-start.13 = (bf16[40,320]{1,0:T(8,128)(2,1)S(1)}, bf16[40,320]{1,0:T(8,128)(2,1)}, u32[]{:S(2)}) copy-start(bf16[40,320]{1,0:T(8,128)(2,1)} %param.16) | copy-start | bytes 76804
  7.9 61.5 %copy-start.15 = (s32[3]{0:T(128)S(1)}, s32[3]{0:T(128)}, u32[]{:S(2)}) copy-start(s32[3]{0:T(128)} %param.11) | copy-start | bytes 40
  7.9 220.7 %all-gather.3.cloned.1.call-start = ((), (), s32[]{:S(2)}) async-start(), calls=%async_computation.1 | async-start | bytes 2488320 | tf_op jit(solution)/shard_map/all_gather | solution.py:90
  8.0 3.6 copy-start.5
  11.5 1.9 copy-start.6
  13.5 56.4 %collective-permute-start = (bf16[2,3,1,128,320]{3,4,2,1,0:T(8,128)(2,1)S(1)}, bf16[2,3,1,128,320]{3,4,2,1,0:T(8,128)(2,1)S(1)}, u32[]{:S(2)}, u32[]{:S(2)}) collective-permute-start(bf16[2,3,1,128,320]{3,4,2,1,0:T(8,128)(2,1)S(1)} %get-tuple-element.14), channel_id=1, source_target_pairs={{0,2},{2,4},{4,6},{6,8},{8,10},{10,12},{12,14},{1,3},{3,5},{5,7},{... | collective-permute-start | bytes 1474568 | tf_op jit(solution)/shard_map/ppermute | solution.py:16
  18.3 51.5 %collective-permute-start.1 = (bf16[2,3,1,128,320]{3,4,2,1,0:T(8,128)(2,1)S(1)}, bf16[2,3,1,128,320]{3,4,2,1,0:T(8,128)(2,1)S(1)}, u32[]{:S(2)}, u32[]{:S(2)}) collective-permute-start(bf16[2,3,1,128,320]{3,4,2,1,0:T(8,128)(2,1)S(1)} %get-tuple-element.15), channel_id=1, source_target_pairs={{2,0},{4,2},{6,4},{8,6},{10,8},{12,10},{14,12},{3,1},{5,3},{7,5},{... | collective-permute-start | bytes 1474568 | tf_op jit(solution)/shard_map/ppermute | solution.py:18
  19.7 344.7 %reduce-scatter.4.cloned.1.call-start = ((), (), s32[]{:S(2)}) async-start(), calls=%async_computation.4 | async-start | bytes 4608000
  94.7 9.1 %copy-start.2 = (bf16[3,18,130,320]{2,3,1,0:T(8,128)(2,1)S(1)}, bf16[3,18,130,320]{2,3,1,0:T(8,128)(2,1)}, u32[]{:S(2)}) copy-start(bf16[3,18,130,320]{2,3,1,0:T(8,128)(2,1)} %get-tuple-element.13) | copy-start | bytes 13478404
  94.7 9.1 %copy-start.9 = (bf16[320,3,3,320]{3,0,2,1:T(8,128)(2,1)S(1)}, bf16[320,3,3,320]{3,0,2,1:T(8,128)(2,1)}, u32[]{:S(2)}) copy-start(bf16[320,3,3,320]{3,0,2,1:T(8,128)(2,1)} %all-gather.5.cloned.1.call-done) | copy-start | bytes 5529604
  177.9 28.4 %copy-start.3 = (bf16[3,16,128,320]{2,3,1,0:T(8,128)(2,1)}, bf16[3,16,128,320]{2,3,1,0:T(8,128)(2,1)S(1)}, u32[]{:S(2)}) copy-start(bf16[3,16,128,320]{2,3,1,0:T(8,128)(2,1)S(1)} %multiply_convert_fusion) | copy-start | bytes 11796484
  178.0 14.5 %slice-start.3 = ((s8[8847360]{0:T(1024)(128)(4,1)}), s8[4194304]{0:T(1024)(128)(4,1)S(1)}, s32[]{:S(2)}) async-start(s8[8847360]{0:T(1024)(128)(4,1)} %bitcast.300), calls=%async_computation.8 | async-start | bytes 8388608
  178.0 14.5 %slice-start.4 = ((s8[8847360]{0:T(1024)(128)(4,1)}), s8[4194304]{0:T(1024)(128)(4,1)S(1)}, s32[]{:S(2)}) async-start(s8[8847360]{0:T(1024)(128)(4,1)} %bitcast.300), calls=%async_computation.9 | async-start | bytes 8388608
  183.7 136.3 %collective-permute-start.2 = (bf16[3,1,128,320]{2,3,1,0:T(8,128)(2,1)S(1)}, bf16[3,1,128,320]{2,3,1,0:T(8,128)(2,1)S(1)}, u32[]{:S(2)}, u32[]{:S(2)}) collective-permute-start(bf16[3,1,128,320]{2,3,1,0:T(8,128)(2,1)S(1)} %get-tuple-element.16), channel_id=1, source_target_pairs={{0,2},{2,4},{4,6},{6,8},{8,10},{10,12},{12,14},{1,3},{3,5},{5,7},{... | collective-permute-start | bytes 737288 | tf_op jit(solution)/shard_map/ppermute | solution.py:16
  185.1 7.5 %slice-start.5 = ((s8[8847360]{0:T(1024)(128)(4,1)}), s8[458752]{0:T(1024)(128)(4,1)S(1)}, s32[]{:S(2)}) async-start(s8[8847360]{0:T(1024)(128)(4,1)} %bitcast.300), calls=%async_computation.10 | async-start | bytes 917504
  185.1 129.7 %collective-permute-start.3 = (bf16[3,1,128,320]{2,3,1,0:T(8,128)(2,1)S(1)}, bf16[3,1,128,320]{2,3,1,0:T(8,128)(2,1)S(1)}, u32[]{:S(2)}, u32[]{:S(2)}) collective-permute-start(bf16[3,1,128,320]{2,3,1,0:T(8,128)(2,1)S(1)} %get-tuple-element.17), channel_id=1, source_target_pairs={{2,0},{4,2},{6,4},{8,6},{10,8},{12,10},{14,12},{3,1},{5,3},{7,5},{... | collective-permute-start | bytes 737288 | tf_op jit(solution)/shard_map/ppermute | solution.py:18
  208.6 2.2 copy-start.10
  216.4 7.6 %copy-start.7 = (bf16[3,16,128,320]{2,3,1,0:T(8,128)(2,1)S(1)}, bf16[3,16,128,320]{2,3,1,0:T(8,128)(2,1)}, u32[]{:S(2)}) copy-start(bf16[3,16,128,320]{2,3,1,0:T(8,128)(2,1)} %get-tuple-element.20) | copy-start | bytes 11796484
  216.4 7.6 %copy-start.14 = (bf16[3,16,128,320]{2,3,1,0:T(8,128)(2,1)S(1)}, bf16[3,16,128,320]{2,3,1,0:T(8,128)(2,1)}, u32[]{:S(2)}) copy-start(bf16[3,16,128,320]{2,3,1,0:T(8,128)(2,1)} %param.17) | copy-start | bytes 11796484
  224.0 2.2 copy-start.8
  228.6 217.7 %all-reduce.5.cloned.1.call-start = ((), (), s32[]{:S(2)}) async-start(), calls=%async_computation.3 | async-start | bytes 1024000 | tf_op jit(solution)/shard_map/psum | solution.py:128
  228.7 9.0 %copy-start.11 = (bf16[320,3,3,320]{3,0,2,1:T(8,128)(2,1)S(1)}, bf16[320,3,3,320]{3,0,2,1:T(8,128)(2,1)}, u32[]{:S(2)}) copy-start(bf16[320,3,3,320]{3,0,2,1:T(8,128)(2,1)} %all-gather.3.cloned.1.call-done) | copy-start | bytes 5529604
  228.7 16.5 %slice-start = ((s8[8847360]{0:T(1024)(128)(4,1)}), s8[4194304]{0:T(1024)(128)(4,1)S(1)}, s32[]{:S(2)}) async-start(s8[8847360]{0:T(1024)(128)(4,1)} %bitcast.298), calls=%async_computation.5 | async-start | bytes 8388608
  228.7 16.5 %slice-start.1 = ((s8[8847360]{0:T(1024)(128)(4,1)}), s8[4194304]{0:T(1024)(128)(4,1)S(1)}, s32[]{:S(2)}) async-start(s8[8847360]{0:T(1024)(128)(4,1)} %bitcast.298), calls=%async_computation.6 | async-start | bytes 8388608
  237.7 7.5 %slice-start.2 = ((s8[8847360]{0:T(1024)(128)(4,1)}), s8[458752]{0:T(1024)(128)(4,1)S(1)}, s32[]{:S(2)}) async-start(s8[8847360]{0:T(1024)(128)(4,1)} %bitcast.298), calls=%async_computation.7 | async-start | bytes 917504
  307.2 7.6 %copy-start.4 = (bf16[3,16,128,320]{2,3,1,0:T(8,128)(2,1)S(1)}, bf16[3,16,128,320]{2,3,1,0:T(8,128)(2,1)}, u32[]{:S(2)}) copy-start(bf16[3,16,128,320]{2,3,1,0:T(8,128)(2,1)} %copy-done.3) | copy-start | bytes 11796484
  359.0 5.4 %copy-start.12 = (s32[3,16,128]{2,1,0:T(8,128)S(1)}, s32[3,16,128]{2,1,0:T(8,128)}, u32[]{:S(2)}) copy-start(s32[3,16,128]{2,1,0:T(8,128)} %param.10) | copy-start | bytes 73732
  364.4 85.8 %copy-start.1 = (bf16[1280,320]{0,1:T(8,128)(2,1)S(1)}, bf16[1280,320]{0,1:T(8,128)(2,1)}, u32[]{:S(2)}) copy-start(bf16[1280,320]{0,1:T(8,128)(2,1)} %param.13) | copy-start | bytes 2457604
Sparse Core Ops, SparseCore 0:
  10.2 66.9 all-gather.4
  79.4 49.2 all-gather.2
  228.7 87.1 reduce-scatter.3
  364.5 20.1 all-reduce.4
where the time goes:
time: 461 us; the launch traced here: 457 us
  matrix products  278 us (60%)
  blocking collectives  107 us (23%)
  other arithmetic  27.1 us (6%)
  local copies, waits for them, and re-layouts  20.2 us (4%)
  between operations  14.4 us (3%)
  starting transfers between devices  9.53 us (2%)
    dot_general x18, matrix products, forward_taps(): jnp.einsum('bhwc,cd->bhwd', frame[:, tap_row:tap_row + row_count, tap_col...  154 us
    psum x1, blocking collectives, per_device(): grad_table = lax.psum(table_local, ('mp', 'dp'))  57.6 us
    dot_general x9, matrix products, backward_taps(): jnp.einsum('bhwd,cd->bhwc', frame[:, 2 - tap_row:2 - tap_row + row_count,...  50.8 us
    all_gather x1, blocking collectives, per_device(): lax.all_gather(mix_weight, 'mp', axis=0, tiled=True)  49.6 us
    dot_general x9, matrix products, per_device(): jnp.einsum('bhwc,bhwd->cd', control_frame[:, tap_row:tap_row + row_count,...  27.3 us
    concatenate x2, other arithmetic, with_halo(): jnp.concatenate([lax.ppermute(tail, axis, [(i, (i + 1) % count) for i in...  24.5 us
    dot_general x1, matrix products, per_device(): jnp.einsum('bhwr,bhwc->rc', onehot.astype(jnp.float32), back_in, precisio...  24.3 us
  transfers between devices with their start and end apart: 8, of which 0 were waited for; matrix products, arithmetic and copies ran while one was open for 69% of the time, Pallas kernels for 0%

commit v1 on v0

--- a/solution.py
+++ b/solution.py
@@ -109,7 +109,7 @@
     table_local = jnp.einsum(
         "bhwr,bhwc->rc", onehot.astype(jnp.float32), back_in, precision=lax.Precision.HIGHEST
     )
-    grad_table = lax.psum(table_local, ("mp", "dp"))
+    grad_table = lax.psum(lax.psum(table_local, "dp"), "mp")
     pieces = []
     for tap_row in range(3):
         for tap_col in range(3):

time: 461 us -> 444 us (0.963)
  blocking collectives: 107 us -> 90.4 us
    psum x1 -> x2, blocking collectives: 57.6 us -> 40.8 us  [per_device(): grad_table = lax.psum(lax.psum(table_local, 'dp'), 'mp')]
  transfers between devices with their start and end apart: 8 -> 8, of which waited for: 0 -> 0; matrix products, arithmetic and copies ran while one was open for 69% -> 72% of each run, Pallas kernels for 0% -> 0%
where the time goes in v1:
time: 444 us; the launch traced here: 440 us
  matrix products  278 us (63%)
  blocking collectives  90.4 us (20%)
  other arithmetic  27.1 us (6%)
  local copies, waits for them, and re-layouts  20.3 us (5%)
  between operations  14.5 us (3%)
  starting transfers between devices  9.53 us (2%)
    dot_general x18, matrix products, forward_taps(): jnp.einsum('bhwc,cd->bhwd', frame[:, tap_row:tap_row + row_count, tap_col...  154 us
    dot_general x9, matrix products, backward_taps(): jnp.einsum('bhwd,cd->bhwc', frame[:, 2 - tap_row:2 - tap_row + row_count,...  50.8 us
    all_gather x1, blocking collectives, per_device(): lax.all_gather(mix_weight, 'mp', axis=0, tiled=True)  49.6 us
    psum x2, blocking collectives, per_device(): grad_table = lax.psum(lax.psum(table_local, 'dp'), 'mp')  40.8 us
    dot_general x9, matrix products, per_device(): jnp.einsum('bhwc,bhwd->cd', control_frame[:, tap_row:tap_row + row_count,...  27.3 us
    concatenate x2, other arithmetic, with_halo(): jnp.concatenate([lax.ppermute(tail, axis, [(i, (i + 1) % count) for i in...  24.5 us
    dot_general x1, matrix products, per_device(): jnp.einsum('bhwr,bhwc->rc', onehot.astype(jnp.float32), back_in, precisio...  24.3 us
  transfers between devices with their start and end apart: 8, of which 0 were waited for; matrix products, arithmetic and copies ran while one was open for 72% of the time, Pallas kernels for 0%

profile of v1, /device:TPU:0, one launch (start us, length us, event | category | flops | bytes accessed | tf_op | source)
XLA Modules:
  0.0 440.2 jit_solution(11632140233852733703)
XLA Ops:
  8.0 3.5 fusion.27
  13.5 4.9 %collective-permute-start = (bf16[2,3,1,128,320]{3,4,2,1,0:T(8,128)(2,1)S(1)}, bf16[2,3,1,128,320]{3,4,2,1,0:T(8,128)(2,1)S(1)}, u32[]{:S(2)}, u32[]{:S(2)}) collective-permute-start(bf16[2,3,1,128,320]{3,4,2,1,0:T(8,128)(2,1)S(1)} %get-tuple-element.14), channel_id=1, source_target_pairs={{0,2},{2,4},{4,6},{6,8},{8,10},{10,12},{12,14},{1,3},{3,5},{5,7},{... | collective-permute-start | bytes 1474568 | tf_op jit(solution)/shard_map/ppermute | solution.py:16
  19.7 49.6 %all_gather.12 = bf16[320,320]{1,0:T(8,128)(2,1)S(1)} all-gather(bf16[40,320]{1,0:T(8,128)(2,1)S(1)} %copy-done.13), channel_id=1, replica_groups=mesh['groups'=2,'mp'=8,'dp'=2] {'mp'}, dimensions={0}, use_global_device_ids=true | all-gather | bytes 230400 | tf_op jit(solution)/shard_map/all_gather | solution.py:94
  69.9 18.2 %select_maximum_fusion = bf16[2,3,18,130,320]{3,4,2,1,0:T(8,128)(2,1)S(1)} fusion(bf16[2,3,1,128,320]{3,4,2,1,0:T(8,128)(2,1)S(1)} %collective-permute-done.1, bf16[2,3,1,128,320]{3,4,2,1,0:T(8,128)(2,1)S(1)} %collective-permute-done, bf16[1,3,16,128,320]{3,4,2,1,0:T(8,128)(2,1)} %copy-done.6, bf16[1,3,16,128,320]{3,4,2,1,0:T(8,128)(2,1)} %bitcast.302), kind=kLoop, calls=%fused_computation.5 | loop fusion | flops 67392000 | bytes 17832960 | tf_op jit(solution)/shard_map/concatenate | solution.py:14
  88.1 6.7 %slice_bitcast_fusion.1 = (bf16[3,18,130,320]{2,3,1,0:T(8,128)(2,1)}, bf16[3,18,130,320]{2,3,1,0:T(8,128)(2,1)}) fusion(bf16[2,3,18,130,320]{3,4,2,1,0:T(8,128)(2,1)S(1)} %select_maximum_fusion), kind=kLoop, calls=%fused_computation.17 | loop fusion | bytes 17971200 | tf_op jit(solution)/shard_map/squeeze | solution.py:84
  94.8 9.1 %fusion.64 = f32[3,16,128,320]{2,3,1,0:T(8,128)} fusion(bf16[3,18,130,320]{2,3,1,0:T(8,128)(2,1)} %get-tuple-element.13, bf16[320,3,3,320]{3,0,2,1:T(8,128)(2,1)} %all-gather.5.cloned.1.call-done), kind=kOutput, calls=%fused_computation.79 | convolution fusion | flops 1258291200 | bytes 12042240 | tf_op jit(solution)/shard_map/bhwc,cd->bhwd/dot_general | solution.py:39
  103.9 5.3 %fusion.68 = f32[3,16,128,320]{2,3,1,0:T(8,128)} fusion(bf16[3,18,130,320]{2,3,1,0:T(8,128)(2,1)S(1)} %copy-done.2, bf16[320,3,3,320]{3,0,2,1:T(8,128)(2,1)S(1)} %copy-done.9), kind=kOutput, calls=%fused_computation.83 | convolution fusion | flops 1258291200 | bytes 12042240 | tf_op jit(solution)/shard_map/bhwc,cd->bhwd/dot_general | solution.py:39
  109.2 5.5 %fusion.72 = f32[3,16,128,320]{2,3,1,0:T(8,128)} fusion(bf16[3,18,130,320]{2,3,1,0:T(8,128)(2,1)S(1)} %copy-done.2, bf16[320,3,3,320]{3,0,2,1:T(8,128)(2,1)S(1)} %copy-done.9), kind=kOutput, calls=%fused_computation.87 | convolution fusion | flops 1258291200 | bytes 12042240 | tf_op jit(solution)/shard_map/bhwc,cd->bhwd/dot_general | solution.py:39
  114.7 5.5 %fusion.76 = f32[3,16,128,320]{2,3,1,0:T(8,128)} fusion(bf16[3,18,130,320]{2,3,1,0:T(8,128)(2,1)S(1)} %copy-done.2, bf16[320,3,3,320]{3,0,2,1:T(8,128)(2,1)S(1)} %copy-done.9), kind=kOutput, calls=%fused_computation.91 | convolution fusion | flops 1258291200 | bytes 12042240 | tf_op jit(solution)/shard_map/bhwc,cd->bhwd/dot_general | solution.py:39
  120.2 5.3 %fusion.80 = f32[3,16,128,320]{2,3,1,0:T(8,128)} fusion(bf16[3,18,130,320]{2,3,1,0:T(8,128)(2,1)S(1)} %copy-done.2, bf16[320,3,3,320]{3,0,2,1:T(8,128)(2,1)S(1)} %copy-done.9), kind=kOutput, calls=%fused_computation.95 | convolution fusion | flops 1258291200 | bytes 12042240 | tf_op jit(solution)/shard_map/bhwc,cd->bhwd/dot_general | solution.py:39
  125.6 5.8 %fusion.84 = f32[3,16,128,320]{2,3,1,0:T(8,128)} fusion(bf16[3,18,130,320]{2,3,1,0:T(8,128)(2,1)S(1)} %copy-done.2, bf16[320,3,3,320]{3,0,2,1:T(8,128)(2,1)S(1)} %copy-done.9), kind=kOutput, calls=%fused_computation.99 | convolution fusion | flops 1258291200 | bytes 12042240 | tf_op jit(solution)/shard_map/bhwc,cd->bhwd/dot_general | solution.py:39
  131.4 5.7 %fusion.88 = f32[3,16,128,320]{2,3,1,0:T(8,128)} fusion(bf16[3,18,130,320]{2,3,1,0:T(8,128)(2,1)S(1)} %copy-done.2, bf16[320,3,3,320]{3,0,2,1:T(8,128)(2,1)S(1)} %copy-done.9), kind=kOutput, calls=%fused_computation.103 | convolution fusion | flops 1258291200 | bytes 12042240 | tf_op jit(solution)/shard_map/bhwc,cd->bhwd/dot_general | solution.py:39
  137.1 5.4 %fusion.92 = f32[3,16,128,320]{2,3,1,0:T(8,128)} fusion(bf16[3,18,130,320]{2,3,1,0:T(8,128)(2,1)S(1)} %copy-done.2, bf16[320,3,3,320]{3,0,2,1:T(8,128)(2,1)S(1)} %copy-done.9), kind=kOutput, calls=%fused_computation.107 | convolution fusion | flops 1258291200 | bytes 12042240 | tf_op jit(solution)/shard_map/bhwc,cd->bhwd/dot_general | solution.py:39
  142.5 28.2 %multiply_convert_fusion.1 = (bf16[3,16,128,320]{2,3,1,0:T(8,128)(2,1)}, f32[3,16,128,320]{2,3,1,0:T(8,128)}) fusion(f32[3,320]{1,0:T(4,128)S(1)} %fusion.163, bf16[3,18,130,320]{2,3,1,0:T(8,128)(2,1)} %get-tuple-element.13, bf16[320,3,3,320]{3,0,2,1:T(8,128)(2,1)S(1)} %copy-done.9, f32[3,16,128,320]{2,3,1,0:T(8,128)} %fusion.64, ...), kind=kOutput, calls=%fused_computation.29 | convolution fusion | flops 1285816320 | bytes 78895104 | tf_op jit(solution)/shard_map/bhwc,cd->bhwd/dot_general | solution.py:39
  170.7 7.3 %multiply_convert_fusion = bf16[3,16,128,320]{2,3,1,0:T(8,128)(2,1)S(1)} fusion(f32[3,16,128,320]{2,3,1,0:T(8,128)} %get-tuple-element.21, bf16[3,16,128,320]{2,3,1,0:T(8,128)(2,1)} %param.17, bf16[320,320]{1,0:T(8,128)(2,1)S(1)} %all_gather.12), kind=kOutput, calls=%fused_computation.27 | convolution fusion | flops 1275985920 | bytes 15933440 | tf_op jit(solution)/shard_map/bhwd,cd->bhwc/dot_general | solution.py:100
  178.1 5.7 %fusion.101 = f32[320,9,320]{0,2,1:T(8,128)S(1)} fusion(bf16[3,16,128,320]{2,3,1,0:T(8,128)(2,1)S(1)} %multiply_convert_fusion, bf16[3,18,130,320]{2,3,1,0:T(8,128)(2,1)} %get-tuple-element.13), kind=kOutput, calls=%fused_computation.110 | convolution fusion | flops 1258291200 | bytes 8355840 | tf_op jit(solution)/shard_map/bhwc,bhwd->cd/dot_general | solution.py:117
  187.1 5.5 %fusion.107 = f32[320,9,320]{0,2,1:T(8,128)S(1)} fusion(f32[320,9,320]{0,2,1:T(8,128)S(1)} %fusion.101, bf16[3,16,128,320]{2,3,1,0:T(8,128)(2,1)S(1)} %multiply_convert_fusion, bf16[3,18,130,320]{2,3,1,0:T(8,128)(2,1)} %get-tuple-element.13), kind=kOutput, calls=%fused_computation.112 | convolution fusion | flops 1258291200 | bytes 8355840 | tf_op jit(solution)/shard_map/bhwc,bhwd->cd/dot_general | solution.py:117
  192.6 2.3 fusion.113
  194.9 2.2 fusion.119
  197.1 2.3 fusion.125
  199.4 2.3 fusion.131
  203.9 2.5 fusion.143
  206.4 2.3 fusion.149
  210.9 5.6 %copy.38 = f32[320,2880]{1,0:T(8,128)} copy(f32[320,2880]{0,1:T(8,128)} %bitcast.304) | data formatting | bytes 7372800 | tf_op jit(solution)/shard_map/reshape | solution.py:124
  216.5 7.6 %fusion.156 = f32[3,16,128,320]{2,3,1,0:T(8,128)} fusion(bf16[3,16,128,320]{2,3,1,0:T(8,128)(2,1)} %get-tuple-element.20, bf16[320,320]{1,0:T(8,128)(2,1)S(1)} %all_gather.12), kind=kOutput, calls=%fused_computation.151 | convolution fusion | flops 1258291200 | bytes 12001280 | tf_op jit(solution)/shard_map/bhwc,cd->bhwd/dot_general | solution.py:98
  226.3 2.3 pad_maximum_fusion
  228.8 9.0 %fusion.42 = f32[3,16,128,320]{2,3,1,0:T(8,128)} fusion(bf16[3,18,130,320]{2,3,1,0:T(8,128)(2,1)} %get-tuple-element.12, bf16[320,3,3,320]{3,0,2,1:T(8,128)(2,1)} %all-gather.3.cloned.1.call-done), kind=kOutput, calls=%fused_computation.57 | convolution fusion | flops 1258291200 | bytes 12042240 | tf_op jit(solution)/shard_map/bhwc,cd->bhwd/dot_general | solution.py:39
  237.7 7.5 %fusion.44 = f32[3,16,128,320]{2,3,1,0:T(8,128)} fusion(bf16[3,18,130,320]{2,3,1,0:T(8,128)(2,1)} %get-tuple-element.12, bf16[320,3,3,320]{3,0,2,1:T(8,128)(2,1)S(1)} %copy-done.11), kind=kOutput, calls=%fused_computation.59 | convolution fusion | flops 1258291200 | bytes 12042240 | tf_op jit(solution)/shard_map/bhwc,cd->bhwd/dot_general | solution.py:39
  245.3 5.5 %fusion.46 = f32[3,16,128,320]{2,3,1,0:T(8,128)} fusion(bf16[3,18,130,320]{2,3,1,0:T(8,128)(2,1)S(1)} %bitcast.299, bf16[320,3,3,320]{3,0,2,1:T(8,128)(2,1)S(1)} %copy-done.11), kind=kOutput, calls=%fused_computation.61 | convolution fusion | flops 1258291200 | bytes 12042240 | tf_op jit(solution)/shard_map/bhwc,cd->bhwd/dot_general | solution.py:39
  250.8 5.6 %fusion.48 = f32[3,16,128,320]{2,3,1,0:T(8,128)} fusion(bf16[3,18,130,320]{2,3,1,0:T(8,128)(2,1)S(1)} %bitcast.299, bf16[320,3,3,320]{3,0,2,1:T(8,128)(2,1)S(1)} %copy-done.11), kind=kOutput, calls=%fused_computation.63 | convolution fusion | flops 1258291200 | bytes 12042240 | tf_op jit(solution)/shard_map/bhwc,cd->bhwd/dot_general | solution.py:39
  256.4 5.3 %fusion.50 = f32[3,16,128,320]{2,3,1,0:T(8,128)} fusion(bf16[3,18,130,320]{2,3,1,0:T(8,128)(2,1)S(1)} %bitcast.299, bf16[320,3,3,320]{3,0,2,1:T(8,128)(2,1)S(1)} %copy-done.11), kind=kOutput, calls=%fused_computation.65 | convolution fusion | flops 1258291200 | bytes 12042240 | tf_op jit(solution)/shard_map/bhwc,cd->bhwd/dot_general | solution.py:39
  261.7 6.0 %fusion.52 = f32[3,16,128,320]{2,3,1,0:T(8,128)} fusion(bf16[3,18,130,320]{2,3,1,0:T(8,128)(2,1)S(1)} %bitcast.299, bf16[320,3,3,320]{3,0,2,1:T(8,128)(2,1)S(1)} %copy-done.11), kind=kOutput, calls=%fused_computation.67 | convolution fusion | flops 1258291200 | bytes 12042240 | tf_op jit(solution)/shard_map/bhwc,cd->bhwd/dot_general | solution.py:39
  267.7 5.5 %fusion.54 = f32[3,16,128,320]{2,3,1,0:T(8,128)} fusion(bf16[3,18,130,320]{2,3,1,0:T(8,128)(2,1)S(1)} %bitcast.299, bf16[320,3,3,320]{3,0,2,1:T(8,128)(2,1)S(1)} %copy-done.11), kind=kOutput, calls=%fused_computation.69 | convolution fusion | flops 1258291200 | bytes 12042240 | tf_op jit(solution)/shard_map/bhwc,cd->bhwd/dot_general | solution.py:39
  273.3 5.3 %fusion.56 = f32[3,16,128,320]{2,3,1,0:T(8,128)} fusion(bf16[3,18,130,320]{2,3,1,0:T(8,128)(2,1)S(1)} %bitcast.299, bf16[320,3,3,320]{3,0,2,1:T(8,128)(2,1)S(1)} %copy-done.11), kind=kOutput, calls=%fused_computation.71 | convolution fusion | flops 1258291200 | bytes 12042240 | tf_op jit(solution)/shard_map/bhwc,cd->bhwd/dot_general | solution.py:39
  278.6 28.7 %add_convert_fusion = bf16[3,16,128,320]{2,3,1,0:T(8,128)(2,1)} fusion(f32[3,16,128,320]{2,3,1,0:T(8,128)} %fusion.156, f32[3,16,128,320]{2,3,1,0:T(8,128)} %fusion.42, f32[3,16,128,320]{2,3,1,0:T(8,128)} %fusion.44, f32[3,16,128,320]{2,3,1,0:T(8,128)} %fusion.46, f32[3,16,128,320]{2,3,1,0:T(8,128)} %fusion.48, f32[3,16,128,320]{2,3,1,0:T(8,128)} %fusion.50, ...), kind=kOutput, calls=%fused_computation.28 | convolution fusion | flops 1287782400 | bytes 78892800 | tf_op jit(solution)/shard_map/bhwc,cd->bhwd/dot_general | solution.py:39
  307.3 7.6 %fusion.158 = f32[3,16,128,320]{2,3,1,0:T(8,128)} fusion(bf16[3,16,128,320]{2,3,1,0:T(8,128)(2,1)} %copy-done.3, bf16[320,3,3,320]{3,0,2,1:T(8,128)(2,1)S(1)} %copy-done.9), kind=kOutput, calls=%fused_computation.153 | convolution fusion | flops 1258291200 | bytes 12042240 | tf_op jit(solution)/shard_map/bhwd,cd->bhwc/dot_general | solution.py:54
  314.9 5.3 %fusion.19 = f32[3,16,128,320]{2,3,1,0:T(8,128)} fusion(bf16[3,1,128,320]{2,3,1,0:T(8,128)(2,1)S(1)} %collective-permute-done.3, bf16[3,16,128,320]{2,3,1,0:T(8,128)(2,1)S(1)} %copy-done.4, bf16[320,3,3,320]{3,0,2,1:T(8,128)(2,1)S(1)} %copy-done.9), kind=kOutput, calls=%fused_computation.33 | convolution fusion | flops 1266647040 | bytes 12288000 | tf_op jit(solution)/shard_map/bhwd,cd->bhwc/dot_general | solution.py:54
  320.2 5.3 %fusion.23 = f32[3,16,128,320]{2,3,1,0:T(8,128)} fusion(bf16[3,16,128,320]{2,3,1,0:T(8,128)(2,1)S(1)} %copy-done.4, bf16[3,1,128,320]{2,3,1,0:T(8,128)(2,1)S(1)} %collective-permute-done.2, bf16[320,3,3,320]{3,0,2,1:T(8,128)(2,1)S(1)} %copy-done.9), kind=kOutput, calls=%fused_computation.37 | convolution fusion | flops 1266647040 | bytes 12288000 | tf_op jit(solution)/shard_map/bhwd,cd->bhwc/dot_general | solution.py:54
  325.5 6.3 %fusion.9 = bf16[3,18,130,320]{2,3,1,0:T(8,128)(2,1)S(1)} fusion(bf16[3,1,128,320]{2,3,1,0:T(8,128)(2,1)S(1)} %collective-permute-done.3, bf16[3,16,128,320]{2,3,1,0:T(8,128)(2,1)S(1)} %copy-done.4, bf16[3,1,128,320]{2,3,1,0:T(8,128)(2,1)S(1)} %collective-permute-done.2), kind=kLoop, calls=%fused_computation.15 | loop fusion | flops 26956800 | bytes 8916480 | tf_op jit(solution)/shard_map/concatenate | solution.py:14
  331.9 5.5 %fusion.30 = f32[3,16,128,320]{2,3,1,0:T(8,128)} fusion(bf16[3,18,130,320]{2,3,1,0:T(8,128)(2,1)S(1)} %fusion.9, bf16[320,3,3,320]{3,0,2,1:T(8,128)(2,1)S(1)} %copy-done.9), kind=kOutput, calls=%fused_computation.45 | convolution fusion | flops 1258291200 | bytes 12042240 | tf_op jit(solution)/shard_map/bhwd,cd->bhwc/dot_general | solution.py:54
  337.4 5.3 %fusion.32 = f32[3,16,128,320]{2,3,1,0:T(8,128)} fusion(bf16[3,18,130,320]{2,3,1,0:T(8,128)(2,1)S(1)} %fusion.9, bf16[320,3,3,320]{3,0,2,1:T(8,128)(2,1)S(1)} %copy-done.9), kind=kOutput, calls=%fused_computation.47 | convolution fusion | flops 1258291200 | bytes 12042240 | tf_op jit(solution)/shard_map/bhwd,cd->bhwc/dot_general | solution.py:54
  342.8 5.5 %fusion.34 = f32[3,16,128,320]{2,3,1,0:T(8,128)} fusion(bf16[3,18,130,320]{2,3,1,0:T(8,128)(2,1)S(1)} %fusion.9, bf16[320,3,3,320]{3,0,2,1:T(8,128)(2,1)S(1)} %copy-done.9), kind=kOutput, calls=%fused_computation.49 | convolution fusion | flops 1258291200 | bytes 12042240 | tf_op jit(solution)/shard_map/bhwd,cd->bhwc/dot_general | solution.py:54
  348.3 5.4 %fusion.36 = f32[3,16,128,320]{2,3,1,0:T(8,128)} fusion(bf16[3,18,130,320]{2,3,1,0:T(8,128)(2,1)S(1)} %fusion.9, bf16[320,3,3,320]{3,0,2,1:T(8,128)(2,1)S(1)} %copy-done.9), kind=kOutput, calls=%fused_computation.51 | convolution fusion | flops 1258291200 | bytes 12042240 | tf_op jit(solution)/shard_map/bhwd,cd->bhwc/dot_general | solution.py:54
  353.7 5.4 %fusion.38 = f32[3,16,128,320]{2,3,1,0:T(8,128)} fusion(bf16[3,18,130,320]{2,3,1,0:T(8,128)(2,1)S(1)} %fusion.9, bf16[320,3,3,320]{3,0,2,1:T(8,128)(2,1)S(1)} %copy-done.9), kind=kOutput, calls=%fused_computation.53 | convolution fusion | flops 1258291200 | bytes 12042240 | tf_op jit(solution)/shard_map/bhwd,cd->bhwc/dot_general | solution.py:54
  359.1 5.3 %fusion.28 = f32[3,16,128,320]{2,3,1,0:T(8,128)} fusion(bf16[3,18,130,320]{2,3,1,0:T(8,128)(2,1)S(1)} %fusion.9, bf16[320,3,3,320]{3,0,2,1:T(8,128)(2,1)S(1)} %copy-done.9), kind=kOutput, calls=%fused_computation.43 | convolution fusion | flops 1258291200 | bytes 12042240 | tf_op jit(solution)/shard_map/bhwd,cd->bhwc/dot_general | solution.py:54
  364.5 24.3 %fusion.152 = f32[16,320]{1,0:T(8,128)S(1)} fusion(f32[3,16,128,320]{2,3,1,0:T(8,128)} %fusion.28, f32[3,16,128,320]{2,3,1,0:T(8,128)} %fusion.23, f32[3,16,128,320]{2,3,1,0:T(8,128)} %fusion.30, f32[3,16,128,320]{2,3,1,0:T(8,128)} %fusion.32, f32[3,16,128,320]{2,3,1,0:T(8,128)} %fusion.158, f32[3,16,128,320]{2,3,1,0:T(8,128)} %fusion.34, ...), kind=kOutput, calls=%fused_computation.128 | convolution fusion | flops 393314304 | bytes 70823936 | tf_op jit(solution)/shard_map/bhwr,bhwc->rc/dot_general | solution.py:109
  388.8 3.4 psum.22
  392.2 37.4 %psum.23 = f32[16,320]{1,0:T(8,128)} all-reduce(f32[16,320]{1,0:T(8,128)S(1)} %psum.22), channel_id=1, replica_groups=mesh['groups'=2,'mp'=8,'dp'=2] {'mp'}, use_global_device_ids=true, to_apply=%region_3.4 | all-reduce | flops 5120 | bytes 40960 | tf_op jit(solution)/shard_map/psum | solution.py:112
  (77 shorter events, 18.3 us)
Async XLA Ops:
  7.2 62.4 %copy-start = (bf16[1280,320]{0,1:T(8,128)(2,1)S(1)}, bf16[1280,320]{0,1:T(8,128)(2,1)}, u32[]{:S(2)}) copy-start(bf16[1280,320]{0,1:T(8,128)(2,1)} %param.13) | copy-start | bytes 2457604
  7.2 87.6 %all-gather.5.cloned.1.call-start = ((), (), s32[]{:S(2)}) async-start(), calls=%async_computation.2 | async-start | bytes 2488320 | tf_op jit(solution)/shard_map/all_gather | solution.py:93
  7.9 11.8 %copy-start.13 = (bf16[40,320]{1,0:T(8,128)(2,1)S(1)}, bf16[40,320]{1,0:T(8,128)(2,1)}, u32[]{:S(2)}) copy-start(bf16[40,320]{1,0:T(8,128)(2,1)} %param.16) | copy-start | bytes 76804
  7.9 61.5 %copy-start.15 = (s32[3]{0:T(128)S(1)}, s32[3]{0:T(128)}, u32[]{:S(2)}) copy-start(s32[3]{0:T(128)} %param.11) | copy-start | bytes 40
  7.9 220.8 %all-gather.3.cloned.1.call-start = ((), (), s32[]{:S(2)}) async-start(), calls=%async_computation.1 | async-start | bytes 2488320 | tf_op jit(solution)/shard_map/all_gather | solution.py:90
  8.0 3.6 copy-start.5
  11.5 1.9 copy-start.6
  13.5 56.4 %collective-permute-start = (bf16[2,3,1,128,320]{3,4,2,1,0:T(8,128)(2,1)S(1)}, bf16[2,3,1,128,320]{3,4,2,1,0:T(8,128)(2,1)S(1)}, u32[]{:S(2)}, u32[]{:S(2)}) collective-permute-start(bf16[2,3,1,128,320]{3,4,2,1,0:T(8,128)(2,1)S(1)} %get-tuple-element.14), channel_id=1, source_target_pairs={{0,2},{2,4},{4,6},{6,8},{8,10},{10,12},{12,14},{1,3},{3,5},{5,7},{... | collective-permute-start | bytes 1474568 | tf_op jit(solution)/shard_map/ppermute | solution.py:16
  18.3 51.5 %collective-permute-start.1 = (bf16[2,3,1,128,320]{3,4,2,1,0:T(8,128)(2,1)S(1)}, bf16[2,3,1,128,320]{3,4,2,1,0:T(8,128)(2,1)S(1)}, u32[]{:S(2)}, u32[]{:S(2)}) collective-permute-start(bf16[2,3,1,128,320]{3,4,2,1,0:T(8,128)(2,1)S(1)} %get-tuple-element.15), channel_id=1, source_target_pairs={{2,0},{4,2},{6,4},{8,6},{10,8},{12,10},{14,12},{3,1},{5,3},{7,5},{... | collective-permute-start | bytes 1474568 | tf_op jit(solution)/shard_map/ppermute | solution.py:18
  19.7 344.8 %reduce-scatter.4.cloned.1.call-start = ((), (), s32[]{:S(2)}) async-start(), calls=%async_computation.4 | async-start | bytes 4608000
  94.8 9.1 %copy-start.2 = (bf16[3,18,130,320]{2,3,1,0:T(8,128)(2,1)S(1)}, bf16[3,18,130,320]{2,3,1,0:T(8,128)(2,1)}, u32[]{:S(2)}) copy-start(bf16[3,18,130,320]{2,3,1,0:T(8,128)(2,1)} %get-tuple-element.13) | copy-start | bytes 13478404
  94.8 9.1 %copy-start.9 = (bf16[320,3,3,320]{3,0,2,1:T(8,128)(2,1)S(1)}, bf16[320,3,3,320]{3,0,2,1:T(8,128)(2,1)}, u32[]{:S(2)}) copy-start(bf16[320,3,3,320]{3,0,2,1:T(8,128)(2,1)} %all-gather.5.cloned.1.call-done) | copy-start | bytes 5529604
  178.0 28.4 %copy-start.3 = (bf16[3,16,128,320]{2,3,1,0:T(8,128)(2,1)}, bf16[3,16,128,320]{2,3,1,0:T(8,128)(2,1)S(1)}, u32[]{:S(2)}) copy-start(bf16[3,16,128,320]{2,3,1,0:T(8,128)(2,1)S(1)} %multiply_convert_fusion) | copy-start | bytes 11796484
  178.1 14.5 %slice-start.3 = ((s8[8847360]{0:T(1024)(128)(4,1)}), s8[4194304]{0:T(1024)(128)(4,1)S(1)}, s32[]{:S(2)}) async-start(s8[8847360]{0:T(1024)(128)(4,1)} %bitcast.300), calls=%async_computation.8 | async-start | bytes 8388608
  178.1 14.5 %slice-start.4 = ((s8[8847360]{0:T(1024)(128)(4,1)}), s8[4194304]{0:T(1024)(128)(4,1)S(1)}, s32[]{:S(2)}) async-start(s8[8847360]{0:T(1024)(128)(4,1)} %bitcast.300), calls=%async_computation.9 | async-start | bytes 8388608
  183.8 136.4 %collective-permute-start.2 = (bf16[3,1,128,320]{2,3,1,0:T(8,128)(2,1)S(1)}, bf16[3,1,128,320]{2,3,1,0:T(8,128)(2,1)S(1)}, u32[]{:S(2)}, u32[]{:S(2)}) collective-permute-start(bf16[3,1,128,320]{2,3,1,0:T(8,128)(2,1)S(1)} %get-tuple-element.16), channel_id=1, source_target_pairs={{0,2},{2,4},{4,6},{6,8},{8,10},{10,12},{12,14},{1,3},{3,5},{5,7},{... | collective-permute-start | bytes 737288 | tf_op jit(solution)/shard_map/ppermute | solution.py:16
  185.2 7.5 %slice-start.5 = ((s8[8847360]{0:T(1024)(128)(4,1)}), s8[458752]{0:T(1024)(128)(4,1)S(1)}, s32[]{:S(2)}) async-start(s8[8847360]{0:T(1024)(128)(4,1)} %bitcast.300), calls=%async_computation.10 | async-start | bytes 917504
  185.2 129.7 %collective-permute-start.3 = (bf16[3,1,128,320]{2,3,1,0:T(8,128)(2,1)S(1)}, bf16[3,1,128,320]{2,3,1,0:T(8,128)(2,1)S(1)}, u32[]{:S(2)}, u32[]{:S(2)}) collective-permute-start(bf16[3,1,128,320]{2,3,1,0:T(8,128)(2,1)S(1)} %get-tuple-element.17), channel_id=1, source_target_pairs={{2,0},{4,2},{6,4},{8,6},{10,8},{12,10},{14,12},{3,1},{5,3},{7,5},{... | collective-permute-start | bytes 737288 | tf_op jit(solution)/shard_map/ppermute | solution.py:18
  208.7 2.2 copy-start.10
  216.5 7.6 %copy-start.7 = (bf16[3,16,128,320]{2,3,1,0:T(8,128)(2,1)S(1)}, bf16[3,16,128,320]{2,3,1,0:T(8,128)(2,1)}, u32[]{:S(2)}) copy-start(bf16[3,16,128,320]{2,3,1,0:T(8,128)(2,1)} %get-tuple-element.20) | copy-start | bytes 11796484
  216.5 7.6 %copy-start.14 = (bf16[3,16,128,320]{2,3,1,0:T(8,128)(2,1)S(1)}, bf16[3,16,128,320]{2,3,1,0:T(8,128)(2,1)}, u32[]{:S(2)}) copy-start(bf16[3,16,128,320]{2,3,1,0:T(8,128)(2,1)} %param.17) | copy-start | bytes 11796484
  224.1 2.2 copy-start.8
  228.7 200.9 %all-reduce.5.cloned.1.call-start = ((), (), s32[]{:S(2)}) async-start(), calls=%async_computation.3 | async-start | bytes 1024000 | tf_op jit(solution)/shard_map/psum | solution.py:128
  228.7 9.0 %copy-start.11 = (bf16[320,3,3,320]{3,0,2,1:T(8,128)(2,1)S(1)}, bf16[320,3,3,320]{3,0,2,1:T(8,128)(2,1)}, u32[]{:S(2)}) copy-start(bf16[320,3,3,320]{3,0,2,1:T(8,128)(2,1)} %all-gather.3.cloned.1.call-done) | copy-start | bytes 5529604
  228.7 16.5 %slice-start = ((s8[8847360]{0:T(1024)(128)(4,1)}), s8[4194304]{0:T(1024)(128)(4,1)S(1)}, s32[]{:S(2)}) async-start(s8[8847360]{0:T(1024)(128)(4,1)} %bitcast.298), calls=%async_computation.5 | async-start | bytes 8388608
  228.8 16.5 %slice-start.1 = ((s8[8847360]{0:T(1024)(128)(4,1)}), s8[4194304]{0:T(1024)(128)(4,1)S(1)}, s32[]{:S(2)}) async-start(s8[8847360]{0:T(1024)(128)(4,1)} %bitcast.298), calls=%async_computation.6 | async-start | bytes 8388608
  237.7 7.5 %slice-start.2 = ((s8[8847360]{0:T(1024)(128)(4,1)}), s8[458752]{0:T(1024)(128)(4,1)S(1)}, s32[]{:S(2)}) async-start(s8[8847360]{0:T(1024)(128)(4,1)} %bitcast.298), calls=%async_computation.7 | async-start | bytes 917504
  307.3 7.6 %copy-start.4 = (bf16[3,16,128,320]{2,3,1,0:T(8,128)(2,1)S(1)}, bf16[3,16,128,320]{2,3,1,0:T(8,128)(2,1)}, u32[]{:S(2)}) copy-start(bf16[3,16,128,320]{2,3,1,0:T(8,128)(2,1)} %copy-done.3) | copy-start | bytes 11796484
  359.1 5.4 %copy-start.12 = (s32[3,16,128]{2,1,0:T(8,128)S(1)}, s32[3,16,128]{2,1,0:T(8,128)}, u32[]{:S(2)}) copy-start(s32[3,16,128]{2,1,0:T(8,128)} %param.10) | copy-start | bytes 73732
  364.5 69.0 %copy-start.1 = (bf16[1280,320]{0,1:T(8,128)(2,1)S(1)}, bf16[1280,320]{0,1:T(8,128)(2,1)}, u32[]{:S(2)}) copy-start(bf16[1280,320]{0,1:T(8,128)(2,1)} %param.13) | copy-start | bytes 2457604
Sparse Core Ops, SparseCore 0:
  10.2 66.9 all-gather.4
  79.4 49.2 all-gather.2
  228.8 86.5 reduce-scatter.3
  364.6 19.8 all-reduce.4
